TPU v7x, 32 devices: a whole 2x2x4 slice. The times are simulated.
32 devices in a mesh: lon: 16 (over z, y, x), lat: 2 (over core).
Axes of the slice: x: 2, y: 2, z: 4, core: 2. Of those that a mesh axis runs over, the one named last changes fastest.
Arguments:
- grid_fields: float32 [48, 1280, 2560], P(None, 'lat', 'lon'), may hold values from -6 to 6
- legendre: bfloat16 [640, 1280, 1281], P('lon', 'lat'), may hold values from -12 to 12
- pair_order: int32 [640], replicated, may hold values from 0 to 639, each once
Outputs:
- spectral: float32 [48, 640, 2, 1281], P('lat', 'lon')
Inputs may be any that keep to these rules, and one draw needn't show every extreme that they name: A permutation; slot s holds wavenumbers pair_order[s] and 1279 - pair_order[s].
All inputs are finite; a program needn't handle non-finite values.
Results may differ from a plain program's by a relative error of at most 0.0029.
Values may be sent and summed in bfloat16 or wider, within the bound.
A program may use at most 320 MiB of HBM per device.

v0:
```python
import math

import jax
import jax.numpy as jnp
from jax import lax
from jax.sharding import PartitionSpec as P

NLON = 2560
M = 1280
NPAIR = 640


def on_device(grid_fields, legendre, pair_order):
    field_count = grid_fields.shape[0]
    slot_count = legendre.shape[0]
    half_rows = M // 2 + 1
    longitude = jnp.arange(NLON, dtype=jnp.int32)
    upper_wave = M - 1 - pair_order
    column_waves = jnp.stack([pair_order, pair_order, upper_wave, upper_wave], axis=1).reshape(-1)
    phase_index = longitude[:, None] * column_waves[None, :] % NLON
    angles = phase_index.astype(jnp.float32) * (2.0 * math.pi / NLON)
    is_cosine = jnp.arange(4 * NPAIR, dtype=jnp.int32) % 2 == 0
    basis_table = jnp.where(is_cosine[None, :], jnp.cos(angles), -jnp.sin(angles)) / NLON
    band_rows = lax.all_to_all(grid_fields, "lon", split_axis=1, concat_axis=2, tiled=True)
    item_count = band_rows.shape[0]
    band_count = band_rows.shape[1]
    flat_rows = band_rows.reshape(item_count * band_count, NLON)
    coef_rows = jnp.dot(
        flat_rows, basis_table, precision=lax.Precision.HIGHEST, preferred_element_type=jnp.float32
    )
    fourier = coef_rows.reshape(item_count, band_count, 4 * NPAIR).astype(jnp.bfloat16)
    owned = lax.all_to_all(fourier, "lon", split_axis=2, concat_axis=1, tiled=True)
    lat_rows = owned.shape[1]
    waves_local = owned.reshape(field_count, lat_rows, slot_count, 4)
    own_pairs = lax.dynamic_slice_in_dim(pair_order, lax.axis_index("lon") * slot_count, slot_count)
    row_index = jnp.arange(half_rows, M + 1, dtype=jnp.int32)
    use_upper = row_index[None, :] >= (M - own_pairs)[:, None]
    lower_table = legendre[:, :, :half_rows]
    upper_table = legendre[:, :, half_rows:]
    share_rows = field_count // lax.axis_size("lat")
    leading = jnp.einsum(
        "fjsc,sjr->fscr", waves_local[..., 0:2], lower_table, preferred_element_type=jnp.float32
    )
    trail_lower = jnp.einsum(
        "fjsc,sjr->fscr", waves_local[..., 0:2], upper_table, preferred_element_type=jnp.float32
    )
    trail_upper = jnp.einsum(
        "fjsc,sjr->fscr", waves_local[..., 2:4], upper_table, preferred_element_type=jnp.float32
    )
    trailing = jnp.where(use_upper[None, :, None, :], trail_upper, trail_lower)
    totals = lax.psum(jnp.concatenate([leading, trailing], axis=3), "lat")
    return lax.dynamic_slice_in_dim(totals, lax.axis_index("lat") * share_rows, share_rows, 0)


def solution(mesh):
    in_specs = (P(None, "lat", "lon"), P("lon", "lat", None), P())
    out_specs = P("lat", "lon", None, None)
    return jax.shard_map(
        on_device, mesh=mesh, in_specs=in_specs, out_specs=out_specs, check_vma=False
    )
```

profile of v0, /device:TPU:0, one launch (start us, length us, event | category | flops | bytes accessed | tf_op | source)
XLA Modules:
  0.0 1590.4 jit_solution(15519590732749291397)
XLA Ops:
  6.5 31.3 %copy.32 = f32[48,640,160]{2,0,1:T(8,128)} copy(f32[48,640,160]{1,2,0:T(8,128)} %param.3) | data formatting | bytes 39321600 | tf_op args[0]
  37.8 0.0 copy-start
  37.8 8.5 all-to-all-start
  46.3 0.0 copy-done
  46.4 0.2 copy.31
  46.6 0.2 mul.28
  46.8 109.8 %fusion.45 = f32[2560,2560]{1,0:T(8,128)} fusion(s32[2560]{0:T(1024)S(1)} %mul.28, pred[2560]{0:T(1024)(128)(4,1)S(1)} %fusion.30), kind=kLoop, calls=%fused_computation.10.clone.clone.clone.1 | loop fusion | flops 78643200 | bytes 26227200 | tf_op jit(solution)/shard_map/dot_general | solution.py:28
  156.6 478.3 %all-to-all-done = f32[48,640,160]{2,0,1:T(8,128)} async-done(((f32[48,640,160]{2,0,1:T(8,128)}), f32[48,640,160]{2,0,1:T(8,128)}, u32[]{:S(2)}, u32[]{:S(2)}) %all-to-all-start) | async-done | bytes 19660832 | tf_op jit(solution)/shard_map/all_to_all | solution.py:24
  634.9 36.1 %copy.34 = f32[48,40,16,160]{3,2,1,0:T(8,128)} copy(f32[48,40,16,160]{3,0,1,2:T(8,128)} %bitcast.2) | data formatting | bytes 39321600 | tf_op jit(solution)/shard_map/all_to_all | solution.py:24
  671.1 32.9 %reshape.51 = f32[1920,2560]{1,0:T(8,128)} reshape(f32[48,40,16,160]{3,2,1,0:T(8,128)} %copy.34) | data formatting | bytes 39321600 | tf_op jit(solution)/shard_map/reshape | solution.py:27
  704.0 165.7 %fusion.24 = bf16[2560,1920]{0,1:T(8,128)(2,1)} fusion(f32[1920,2560]{1,0:T(8,128)} %reshape.51, f32[2560,2560]{1,0:T(8,128)} %fusion.45), kind=kOutput, calls=%fused_computation.26 | convolution fusion | flops 150999859200 | bytes 55705600 | tf_op jit(solution)/shard_map/dot_general | solution.py:28
  869.7 29.9 %copy.35 = bf16[48,40,2560]{0,1,2:T(8,128)(2,1)} copy(bf16[48,40,2560]{2,1,0:T(8,128)(2,1)} %bitcast.46) | data formatting | bytes 19660800 | tf_op jit(solution)/shard_map/convert_element_type | solution.py:31
  899.6 40.3 %reshape.55 = bf16[16,2,153600]{2,1,0:T(2,128)(2,1)} reshape(bf16[2560,40,48]{2,1,0:T(8,128)(2,1)} %bitcast.44) | data formatting | bytes 19660800
  939.9 140.1 %all-to-all-start.1 = ((bf16[16,2,153600]{2,1,0:T(2,128)(2,1)}), bf16[16,2,153600]{2,1,0:T(2,128)(2,1)}, u32[]{:S(2)}, u32[]{:S(2)}) async-start(bf16[16,2,153600]{2,1,0:T(2,128)(2,1)} %reshape.55), calls=%async_computation.1 | async-start | bytes 19660800 | tf_op jit(solution)/shard_map/all_to_all | solution.py:32
  1080.0 0.0 all-reduce.2.cloned.1.call-start
  1080.1 22.9 %slice.16 = bf16[40,640,640]{1,0,2:T(8,128)(2,1)} slice(bf16[40,640,1281]{1,0,2:T(8,128)(2,1)} %param.4), slice={[0:40], [0:640], [641:1281]} | slice | bytes 65536000 | tf_op jit(solution)/shard_map/slice | solution.py:39
  1103.0 22.7 %slice.14 = bf16[40,640,641]{1,0,2:T(8,128)(2,1)} slice(bf16[40,640,1281]{1,0,2:T(8,128)(2,1)} %param.4), slice={[0:40], [0:640], [0:641]} | slice | bytes 65638400 | tf_op jit(solution)/shard_map/slice | solution.py:38
  1125.7 51.4 %copy.47 = bf16[40,640,640]{2,1,0:T(8,128)(2,1)} copy(bf16[40,640,640]{1,0,2:T(8,128)(2,1)} %slice.16) | data formatting | bytes 65536000
  1177.2 0.8 dynamic-slice_subtract_fusion
  1177.9 0.1 broadcast_compare_fusion
  1178.0 82.2 %all-to-all-done.1 = bf16[16,2,153600]{2,1,0:T(2,128)(2,1)} async-done(((bf16[16,2,153600]{2,1,0:T(2,128)(2,1)}), bf16[16,2,153600]{2,1,0:T(2,128)(2,1)}, u32[]{:S(2)}, u32[]{:S(2)}) %all-to-all-start.1) | async-done | bytes 9830432 | tf_op jit(solution)/shard_map/all_to_all | solution.py:32
  1260.2 27.6 %reshape.56 = bf16[2560,40,48]{2,1,0:T(8,128)(2,1)} reshape(bf16[16,2,153600]{2,1,0:T(2,128)(2,1)} %all-to-all-done.1) | data formatting | bytes 19660800
  1287.9 41.1 %copy.37 = bf16[48,16,40,160]{2,1,0,3:T(8,128)(2,1)} copy(bf16[48,16,40,160]{0,2,3,1:T(8,128)(2,1)} %bitcast.45) | data formatting | bytes 19660800 | tf_op jit(solution)/shard_map/all_to_all | solution.py:32
  1329.0 43.4 %reshape.52 = bf16[48,640,40,4]{1,0,3,2:T(8,128)(2,1)} reshape(bf16[48,16,40,160]{2,1,0,3:T(8,128)(2,1)} %copy.37) | data formatting | bytes 19660800 | tf_op jit(solution)/shard_map/reshape | solution.py:34
  1372.4 21.6 %fusion.1 = f32[40,48,2,640]{3,1,2,0:T(8,128)} fusion(bf16[48,640,40,4]{1,0,3,2:T(8,128)(2,1)} %reshape.52, bf16[40,640,640]{2,1,0:T(8,128)(2,1)} %copy.47), kind=kOutput, calls=%fused_computation.3 | convolution fusion | flops 3145728000 | bytes 52428800 | tf_op jit(solution)/shard_map/fjsc,sjr->fscr/dot_general | solution.py:44
  1394.0 24.9 %fusion.27 = f32[48,40,2,641]{3,0,2,1:T(8,128)} fusion(bf16[48,640,40,4]{1,0,3,2:T(8,128)(2,1)} %reshape.52, bf16[40,640,641]{1,0,2:T(8,128)(2,1)} %slice.14), kind=kOutput, calls=%fused_computation.28 | convolution fusion | flops 3150643200 | bytes 52495360 | tf_op jit(solution)/shard_map/fjsc,sjr->fscr/dot_general | solution.py:41
  1418.9 21.6 %select_bitcast_fusion = f32[48,40,2,640]{3,0,2,1:T(8,128)} fusion(f32[40,48,2,640]{3,1,2,0:T(8,128)} %fusion.1, pred[40,640]{1,0:T(8,128)(4,1)S(1)} %broadcast_compare_fusion, bf16[48,640,40,4]{1,0,3,2:T(8,128)(2,1)} %reshape.52, bf16[40,640,640]{2,1,0:T(8,128)(2,1)} %copy.47), kind=kOutput, calls=%fused_computation.27 | convolution fusion | flops 3148185600 | bytes 62284800 | tf_op jit(solution)/shard_map/fjsc,sjr->fscr/dot_general | solution.py:47
  1440.6 17.8 %pad_maximum_fusion = f32[48,40,2,1281]{3,0,2,1:T(8,128)} fusion(f32[48,40,2,640]{3,0,2,1:T(8,128)} %select_bitcast_fusion, f32[48,40,2,641]{3,0,2,1:T(8,128)} %fusion.27), kind=kLoop, calls=%fused_computation.19 | loop fusion | flops 4919040 | bytes 39352320 | tf_op jit(solution)/shard_map/concatenate | solution.py:51
  1458.3 0.0 all-reduce.2.cloned.1.call-update
  1458.4 112.5 %all-reduce.2.cloned.1.call-done = f32[48,40,2,1281]{3,0,2,1:T(8,128)} async-done(((f32[48,40,2,1281]{3,0,2,1:T(8,128)}), f32[48,40,2,1281]{3,0,2,1:T(8,128)}) %all-reduce.2.cloned.1.call-update) | async-done | bytes 19676176 | tf_op jit(solution)/shard_map/psum | solution.py:51
  1570.9 4.8 constant_dynamic-slice_fusion
  1575.7 7.4 copy.40
  (6 shorter events, 0.0 us)
Async XLA Ops:
  37.8 8.5 copy-start
  37.8 597.1 %all-to-all-start = ((f32[48,640,160]{2,0,1:T(8,128)}), f32[48,640,160]{2,0,1:T(8,128)}, u32[]{:S(2)}, u32[]{:S(2)}) async-start(f32[48,640,160]{2,0,1:T(8,128)} %copy.32), calls=%async_computation | async-start | bytes 62914560 | tf_op jit(solution)/shard_map/all_to_all | solution.py:24
  939.9 320.3 %all-to-all-start.1 = ((bf16[16,2,153600]{2,1,0:T(2,128)(2,1)}), bf16[16,2,153600]{2,1,0:T(2,128)(2,1)}, u32[]{:S(2)}, u32[]{:S(2)}) async-start(bf16[16,2,153600]{2,1,0:T(2,128)(2,1)} %reshape.55), calls=%async_computation.1 | async-start | bytes 19660800 | tf_op jit(solution)/shard_map/all_to_all | solution.py:32
  1080.0 490.9 %all-reduce.2.cloned.1.call-start = ((), (), s32[]{:S(2)}) async-start(), calls=%async_computation.2 | async-start | bytes 43253760 | tf_op jit(solution)/shard_map/psum | solution.py:51
Sparse Core Ops, SparseCore 0:
  1458.5 112.3 all-reduce.1
where the time goes:
time: 1600 us; the launch traced here: 1590 us
  waiting for transfers between devices  673 us (42%)
  local copies, waits for them, and re-layouts  392 us (24%)
  matrix products  234 us (15%)
  starting transfers between devices  149 us (9%)
  other arithmetic  128 us (8%)
    all_to_all x1, waiting for transfers between devices, on_device(): lax.all_to_all(grid_fields, 'lon', split_axis=1, concat_axis=2, tiled=True)  478 us
    dot_general x1, matrix products, on_device(): jnp.dot(flat_rows, basis_table, precision=lax.Precision.HIGHEST, preferre...  166 us
    unnamed x6, local copies, waits for them, and re-layouts  151 us
    all_to_all x1, starting transfers between devices, on_device(): lax.all_to_all(fourier, 'lon', split_axis=2, concat_axis=1, tiled=True)  140 us
    psum x1, waiting for transfers between devices, on_device(): totals = lax.psum(jnp.concatenate([leading, trailing], axis=3), 'lat')  113 us
    dot_general x1, other arithmetic, on_device(): jnp.dot(flat_rows, basis_table, precision=lax.Precision.HIGHEST, preferre...  110 us
    all_to_all x1, waiting for transfers between devices, on_device(): lax.all_to_all(fourier, 'lon', split_axis=2, concat_axis=1, tiled=True)  82.2 us
    reshape x1, local copies, waits for them, and re-layouts, on_device(): waves_local = owned.reshape(field_count, lat_rows, slot_count, 4)  43.4 us
  transfers between devices with their start and end apart: 3, of which 3 were waited for; matrix products, arithmetic and copies ran while one was open for 13% of the time, Pallas kernels for 0%

commit v1 on v0

v1 whole, which is shorter than its diff:
```python
import math

import jax
import jax.numpy as jnp
from jax import lax
from jax.sharding import PartitionSpec as P

NLON = 2560
M = 1280
NPAIR = 640
WIRE = jnp.float16
WIRE_SCALE = 8192.0
FINE = 64


def basis(pair_order):
    upper_wave = M - 1 - pair_order
    waves = jnp.stack([pair_order, pair_order, upper_wave, upper_wave], axis=1).reshape(-1)
    shift = (jnp.arange(4 * NPAIR, dtype=jnp.int32) % 2) * (NLON // 4)
    coarse = (waves[:, None] * (FINE * jnp.arange(NLON // FINE, dtype=jnp.int32))[None, :] + shift[:, None]) % NLON
    fine = waves[:, None] * jnp.arange(FINE, dtype=jnp.int32)[None, :] % NLON
    unit = 2.0 * math.pi / NLON
    coarse = coarse.astype(jnp.float32) * unit
    fine = fine.astype(jnp.float32) * unit
    norm = 1.0 / (NLON * WIRE_SCALE)
    ca, sa = jnp.cos(coarse) * norm, jnp.sin(coarse) * norm
    cb, sb = jnp.cos(fine), jnp.sin(fine)
    ca, sa, cb, sb = lax.optimization_barrier((ca, sa, cb, sb))
    table = ca[:, :, None] * cb[:, None, :] - sa[:, :, None] * sb[:, None, :]
    return table.reshape(4 * NPAIR, NLON)


def on_device(grid_fields, legendre, pair_order):
    field_count, band, lon_local = grid_fields.shape
    slots = legendre.shape[0]
    devices = lax.axis_size("lon")
    half_rows = M // 2 + 1
    split_f = math.gcd(field_count, devices)
    split_l = devices // split_f
    chunks = field_count // split_f
    part = band // split_l

    by_lon = jnp.transpose(grid_fields, (0, 2, 1))
    received = []
    for i in range(chunks):
        own = by_lon[i * split_f:(i + 1) * split_f]
        own = (own * WIRE_SCALE).astype(WIRE)
        own = own.reshape(split_f, lon_local, split_l, part).transpose(0, 2, 1, 3)
        own = own.reshape(devices, lon_local, part)
        received.append(lax.all_to_all(own, "lon", split_axis=0, concat_axis=0, tiled=True))
    table = basis(pair_order)
    waves = []
    for i in range(chunks):
        rows = received[i].reshape(NLON, part).astype(jnp.float32)
        coef = jnp.dot(table, rows, precision=lax.Precision.HIGH, preferred_element_type=jnp.float32)
        fourier = coef.astype(jnp.bfloat16).reshape(devices, slots * 4, part)
        owned = lax.all_to_all(fourier, "lon", split_axis=0, concat_axis=0, tiled=True)
        owned = owned.reshape(split_f, split_l, slots * 4, part).transpose(0, 2, 1, 3)
        waves.append(owned.reshape(split_f, slots, 4, band))
    waves_local = jnp.concatenate(waves, axis=0)

    own_pairs = lax.dynamic_slice_in_dim(pair_order, lax.axis_index("lon") * slots, slots)
    row_index = jnp.arange(half_rows, M + 1, dtype=jnp.int32)
    use_upper = row_index[None, :] >= (M - own_pairs)[:, None]
    turned = lax.optimization_barrier(jnp.transpose(legendre, (0, 2, 1)))
    lower_table = turned[:, :half_rows]
    upper_table = turned[:, half_rows:]
    lower = jnp.transpose(waves_local[:, :, 0:2], (1, 0, 2, 3)).reshape(slots, field_count * 2, band)
    upper = jnp.transpose(waves_local[:, :, 2:4], (1, 0, 2, 3)).reshape(slots, field_count * 2, band)

    def sums(w, t):
        return lax.dot_general(w, t, (((2,), (2,)), ((0,), (0,))), preferred_element_type=jnp.float32)

    leading = sums(lower, lower_table)
    trailing = jnp.where(use_upper[:, None, :], sums(upper, upper_table), sums(lower, upper_table))
    totals = jnp.concatenate([leading, trailing], axis=2)
    totals = totals.reshape(slots, field_count, 2, M + 1).transpose(1, 0, 2, 3)
    return lax.psum_scatter(totals, "lat", scatter_dimension=0, tiled=True)


def solution(mesh):
    in_specs = (P(None, "lat", "lon"), P("lon", "lat", None), P())
    out_specs = P("lat", "lon", None, None)
    return jax.shard_map(
        on_device, mesh=mesh, in_specs=in_specs, out_specs=out_specs, check_vma=False
    )
```

time: 1600 us -> 682 us (0.43)
  waiting for transfers between devices: 673 us -> 91.9 us
  local copies, waits for them, and re-layouts: 392 us -> 145 us
  blocking collectives: 0 us -> 161 us
  starting transfers between devices: 149 us -> 48.2 us
  other arithmetic: 128 us -> 31.4 us
  matrix products: 234 us -> 184 us
    all_to_all x2 -> x4, waiting for transfers between devices: 561 us -> 51.4 us  [the longest x3 45.4 us: on_device(): lax.all_to_all(fourier, 'lon', split_axis=0, concat_axis=0, tiled=True)]
    all_to_all x0 -> x2, blocking collectives: none -> 161 us  [on_device(): lax.all_to_all(own, 'lon', split_axis=0, concat_axis=0, tiled=True)]
    psum x1 -> x0, waiting for transfers between devices: 113 us -> none  [on_device(): totals = lax.psum(jnp.concatenate([leading, trailing], axis=3), 'lat')]
    dot_general x1 -> x0, other arithmetic: 110 us -> none  [on_device(): jnp.dot(flat_rows, basis_table, precision=lax.Precision.HIGHEST, preferre...]
    all_to_all x2 -> x4, starting transfers between devices: 149 us -> 48.2 us  [the longest x3 44.4 us: on_device(): lax.all_to_all(fourier, 'lon', split_axis=0, concat_axis=0, tiled=True)]
    unnamed x6 -> x11, local copies, waits for them, and re-layouts: 151 us -> 53.4 us
    all_to_all x2 -> x0, local copies, waits for them, and re-layouts: 77.3 us -> none  [the longest x1 41.1 us: on_device(): lax.all_to_all(fourier, 'lon', split_axis=2, concat_axis=1, tiled=True)]
    dot_general x4 -> x6, matrix products: 234 us -> 184 us  [the longest x3 122 us: on_device(): jnp.dot(table, rows, precision=lax.Precision.HIGH, preferred_element_type...]
  transfers between devices with their start and end apart: 3 -> 5, of which waited for: 3 -> 5; matrix products, arithmetic and copies ran while one was open for 13% -> 30% of each run, Pallas kernels for 0% -> 0%
where the time goes in v1:
time: 682 us; the launch traced here: 675 us
  matrix products  184 us (27%)
  blocking collectives  161 us (24%)
  local copies, waits for them, and re-layouts  145 us (21%)
  waiting for transfers between devices  91.9 us (13%)
  starting transfers between devices  48.2 us (7%)
  other arithmetic  31.4 us (5%)
  between operations  14 us (2%)
    all_to_all x2, blocking collectives, on_device(): lax.all_to_all(own, 'lon', split_axis=0, concat_axis=0, tiled=True)  161 us
    dot_general x3, matrix products, on_device(): jnp.dot(table, rows, precision=lax.Precision.HIGH, preferred_element_type...  122 us
    dot_general x3, matrix products, sums(): lax.dot_general(w, t, (((2,), (2,)), ((0,), (0,))), preferred_element_typ...  61.4 us
    unnamed x11, local copies, waits for them, and re-layouts  53.4 us
    all_to_all x3, waiting for transfers between devices, on_device(): lax.all_to_all(fourier, 'lon', split_axis=0, concat_axis=0, tiled=True)  45.4 us
    all_to_all x3, starting transfers between devices, on_device(): lax.all_to_all(fourier, 'lon', split_axis=0, concat_axis=0, tiled=True)  44.4 us
    reduce_scatter x1, waiting for transfers between devices, on_device(): return lax.psum_scatter(totals, 'lat', scatter_dimension=0, tiled=True)  40.5 us
    reduce_scatter x1, local copies, waits for them, and re-layouts, on_device(): return lax.psum_scatter(totals, 'lat', scatter_dimension=0, tiled=True)  16.4 us
  transfers between devices with their start and end apart: 5, of which 5 were waited for; matrix products, arithmetic and copies ran while one was open for 30% of the time, Pallas kernels for 0%

profile of v1, /device:TPU:0, one launch (start us, length us, event | category | flops | bytes accessed | tf_op | source)
XLA Modules:
  0.0 674.7 jit_solution(8264189601384991449)
XLA Ops:
  6.5 9.5 %fusion.6 = (f16[16,160,640]{2,1,0:T(8,128)(2,1)S(1)}, f16[16,160,640]{2,1,0:T(8,128)(2,1)S(1)}, f16[16,160,640]{2,1,0:T(8,128)(2,1)}) fusion(f32[48,160,640]{2,1,0:T(8,128)} %bitcast.34), kind=kLoop, calls=%fused_computation.10 | loop fusion | flops 9830400 | bytes 29491200 | tf_op jit(solution)/shard_map/convert_element_type | solution.py:47
  16.0 83.1 %all_to_all.30 = f16[16,160,640]{2,1,0:T(8,128)(2,1)} all-to-all(f16[16,160,640]{2,1,0:T(8,128)(2,1)S(1)} %get-tuple-element.13), channel_id=1, replica_groups=mesh['lon'=16,'lat'=2] {'lon'}, dimensions={0} | all-to-all | bytes 6553600 | tf_op jit(solution)/shard_map/all_to_all | solution.py:50
  99.1 0.0 copy-start.3
  99.2 77.8 %all_to_all.31 = f16[16,160,640]{2,1,0:T(8,128)(2,1)} all-to-all(f16[16,160,640]{2,1,0:T(8,128)(2,1)S(1)} %get-tuple-element.14), channel_id=1, replica_groups=mesh['lon'=16,'lat'=2] {'lon'}, dimensions={0} | all-to-all | bytes 6553600 | tf_op jit(solution)/shard_map/all_to_all | solution.py:50
  177.0 3.7 all-to-all-start
  180.7 0.0 copy-done.3
  180.8 0.9 copy.15
  181.7 1.2 mul.136
  182.9 1.8 sine_multiply_fusion
  184.6 2.6 fusion.15
  187.3 0.0 copy-start.2
  187.3 9.4 %multiply_subtract_fusion = f32[2560,40,64]{0,2,1:T(8,128)} fusion(f32[2560,64]{0,1:T(8,128)S(1)} %get-tuple-element.12, f32[2560,40]{0,1:T(8,128)S(1)} %get-tuple-element.11, f32[2560,64]{0,1:T(8,128)S(1)} %get-tuple-element.10, f32[2560,40]{0,1:T(8,128)S(1)} %get-tuple-element.9), kind=kLoop, calls=%fused_computation.7 | loop fusion | flops 19660800 | bytes 28344320 | tf_op jit(solution)/shard_map/sub | solution.py:29
  196.7 0.0 copy-done.2
  196.7 40.5 %convolution_convert_fusion.1 = bf16[2560,640]{1,0:T(8,128)(2,1)} fusion(f32[2560,2560]{0,1:T(8,128)} %bitcast.31, f16[2560,640]{1,0:T(8,128)(2,1)S(1)} %bitcast.38), kind=kOutput, calls=%fused_computation.19 | convolution fusion | flops 25167462400 | bytes 32768000 | tf_op jit(solution)/shard_map/dot_general | solution.py:55
  237.2 6.1 all-to-all-done
  243.3 0.0 copy-start.1
  243.3 1.7 copy-done.1
  245.0 15.0 %all-to-all-start.3 = ((bf16[16,160,640]{2,1,0:T(8,128)(2,1)}), bf16[16,160,640]{2,1,0:T(8,128)(2,1)S(1)}, u32[]{:S(2)}, u32[]{:S(2)}) async-start(bf16[16,160,640]{2,1,0:T(8,128)(2,1)} %bitcast.40), calls=%async_computation.3 | async-start | bytes 6553600 | tf_op jit(solution)/shard_map/all_to_all | solution.py:57
  260.0 40.8 %convolution_convert_fusion.2 = bf16[2560,640]{1,0:T(8,128)(2,1)} fusion(f32[2560,2560]{0,1:T(8,128)} %bitcast.32, f16[2560,640]{1,0:T(8,128)(2,1)} %bitcast.37), kind=kOutput, calls=%fused_computation.20 | convolution fusion | flops 25167462400 | bytes 32768000 | tf_op jit(solution)/shard_map/dot_general | solution.py:55
  300.8 22.0 %all-to-all-done.3 = bf16[16,160,640]{2,1,0:T(8,128)(2,1)S(1)} async-done(((bf16[16,160,640]{2,1,0:T(8,128)(2,1)}), bf16[16,160,640]{2,1,0:T(8,128)(2,1)S(1)}, u32[]{:S(2)}, u32[]{:S(2)}) %all-to-all-start.3) | async-done | bytes 3276832 | tf_op jit(solution)/shard_map/all_to_all | solution.py:57
  322.8 14.8 %all-to-all-start.1 = ((bf16[16,160,640]{2,1,0:T(8,128)(2,1)}), bf16[16,160,640]{2,1,0:T(8,128)(2,1)}, u32[]{:S(2)}, u32[]{:S(2)}) async-start(bf16[16,160,640]{2,1,0:T(8,128)(2,1)} %bitcast.39), calls=%async_computation.1 | async-start | bytes 6553600 | tf_op jit(solution)/shard_map/all_to_all | solution.py:57
  337.6 40.8 %convolution_convert_fusion = bf16[2560,640]{1,0:T(8,128)(2,1)} fusion(f32[2560,2560]{0,1:T(8,128)} %bitcast.33, f16[2560,640]{1,0:T(8,128)(2,1)} %bitcast.35), kind=kOutput, calls=%fused_computation.18 | convolution fusion | flops 25167462400 | bytes 32768000 | tf_op jit(solution)/shard_map/dot_general | solution.py:55
  378.4 22.0 %all-to-all-done.1 = bf16[16,160,640]{2,1,0:T(8,128)(2,1)} async-done(((bf16[16,160,640]{2,1,0:T(8,128)(2,1)}), bf16[16,160,640]{2,1,0:T(8,128)(2,1)}, u32[]{:S(2)}, u32[]{:S(2)}) %all-to-all-start.1) | async-done | bytes 3276832 | tf_op jit(solution)/shard_map/all_to_all | solution.py:57
  400.5 14.6 %all-to-all-start.5 = ((bf16[16,160,640]{2,1,0:T(8,128)(2,1)}), bf16[16,160,640]{2,1,0:T(8,128)(2,1)}, u32[]{:S(2)}, u32[]{:S(2)}) async-start(bf16[16,160,640]{2,1,0:T(8,128)(2,1)} %bitcast.36), calls=%async_computation.5 | async-start | bytes 6553600 | tf_op jit(solution)/shard_map/all_to_all | solution.py:57
  415.1 0.0 reduce-scatter.2.cloned.1.call-start
  415.2 44.1 %copy.29 = bf16[40,640,1281]{1,2,0:T(8,128)(2,1)} copy(bf16[40,640,1281]{1,0,2:T(8,128)(2,1)} %param.4) | data formatting | bytes 131174400 | tf_op args[1]
  459.3 0.1 dynamic-slice_subtract_fusion
  459.3 0.1 broadcast_compare_fusion
  459.4 3.1 reshape_transpose_reshape.10
  462.5 0.0 copy-start
  462.5 6.6 reshape_transpose_reshape.9
  469.1 4.8 constant_dynamic-update-slice_fusion.2
  473.9 0.0 copy-done
  473.9 2.8 constant_dynamic-update-slice_fusion.1
  476.7 1.4 all-to-all-done.5
  478.1 5.4 reshape_transpose_reshape.11
  483.5 2.8 constant_dynamic-update-slice_fusion
  486.3 10.3 %fusion.27 = (bf16[48,40,2,640]{3,2,1,0:T(2,128)(2,1)S(1)}, bf16[48,40,2,640]{3,2,1,0:T(2,128)(2,1)S(1)}) fusion(bf16[48,40,4,640]{3,2,1,0:T(4,128)(2,1)} %constant_dynamic-update-slice_fusion), kind=kLoop, calls=%fused_computation.54 | loop fusion | bytes 19660800 | tf_op jit(solution)/shard_map/slice | solution.py:69
  496.6 7.9 %copy_bitcast_fusion.1 = (bf16[40,48,2,640]{3,2,1,0:T(2,128)(2,1)}, bf16[40,48,2,640]{3,2,1,0:T(2,128)(2,1)}) fusion(bf16[48,40,2,640]{3,2,1,0:T(2,128)(2,1)S(1)} %get-tuple-element.16, bf16[48,40,2,640]{3,2,1,0:T(2,128)(2,1)S(1)} %get-tuple-element.17), kind=kLoop, calls=%fused_computation.15 | loop fusion | bytes 19660800 | tf_op jit(solution)/shard_map/transpose | solution.py:69
  504.5 11.0 %reshape.108 = bf16[40,96,640]{2,1,0:T(8,128)(2,1)} reshape(bf16[40,48,2,640]{3,2,1,0:T(2,128)(2,1)} %get-tuple-element.23) | data formatting | bytes 9830400 | tf_op jit(solution)/shard_map/reshape | solution.py:68
  515.5 20.4 %fusion.2 = f32[40,96,640]{2,1,0:T(8,128)} fusion(bf16[40,96,640]{2,1,0:T(8,128)(2,1)} %reshape.108, bf16[40,1281,640]{2,1,0:T(8,128)(2,1)} %bitcast.27), kind=kOutput, calls=%fused_computation.3 | convolution fusion | flops 3145728000 | bytes 47513600 | tf_op jit(solution)/shard_map/dot_general | solution.py:72
  535.9 21.5 %fusion = f32[40,96,641]{2,1,0:T(8,128)} fusion(bf16[40,96,640]{2,1,0:T(8,128)(2,1)} %reshape.108, bf16[40,1281,640]{2,1,0:T(8,128)(2,1)} %bitcast.28), kind=kOutput, calls=%fused_computation.1 | convolution fusion | flops 3150643200 | bytes 47938560 | tf_op jit(solution)/shard_map/dot_general | solution.py:72
  557.4 11.0 %reshape.109 = bf16[40,96,640]{2,1,0:T(8,128)(2,1)} reshape(bf16[40,48,2,640]{3,2,1,0:T(2,128)(2,1)} %get-tuple-element.22) | data formatting | bytes 9830400 | tf_op jit(solution)/shard_map/reshape | solution.py:69
  568.4 19.5 %broadcast_select_fusion = f32[40,96,640]{2,1,0:T(8,128)S(1)} fusion(f32[40,96,640]{2,1,0:T(8,128)} %fusion.2, pred[40,640]{1,0:T(8,128)(4,1)S(1)} %broadcast_compare_fusion, bf16[40,96,640]{2,1,0:T(8,128)(2,1)} %reshape.109, bf16[40,1281,640]{2,1,0:T(8,128)(2,1)} %bitcast.29), kind=kOutput, calls=%fused_computation.17 | convolution fusion | flops 3148185600 | bytes 57369600 | tf_op jit(solution)/shard_map/dot_general | solution.py:72
  587.9 7.9 %pad_maximum_fusion = f32[40,96,1281]{2,1,0:T(8,128)S(1)} fusion(f32[40,96,640]{2,1,0:T(8,128)S(1)} %broadcast_select_fusion, f32[40,96,641]{2,1,0:T(8,128)} %fusion), kind=kLoop, calls=%fused_computation.8 | loop fusion | flops 4919040 | bytes 39352320 | tf_op jit(solution)/shard_map/concatenate | solution.py:76
  595.8 14.7 %copy.23 = f32[40,96,1281]{2,0,1:T(8,128)} copy(f32[40,96,1281]{2,1,0:T(8,128)S(1)} %pad_maximum_fusion) | data formatting | bytes 39352320 | tf_op jit(solution)/shard_map/reshape | solution.py:77
  610.5 0.0 reduce-scatter.2.cloned.1.call-update
  610.5 40.5 %reduce-scatter.2.cloned.1.call-done = f32[24,40,2,1281]{3,1,2,0:T(8,128)} async-done(((f32[48,40,2,1281]{3,1,2,0:T(8,128)}), f32[24,40,2,1281]{3,1,2,0:T(8,128)}) %reduce-scatter.2.cloned.1.call-update) | async-done | bytes 9838096 | tf_op jit(solution)/shard_map/reduce_scatter | solution.py:78
  651.0 16.4 %copy.21 = f32[24,40,2,1281]{3,2,1,0:T(2,128)} copy(f32[24,40,2,1281]{3,1,2,0:T(8,128)} %reduce-scatter.2.cloned.1.call-done) | data formatting | bytes 19676160 | tf_op jit(solution)/shard_map/reduce_scatter | solution.py:78
  (7 shorter events, 0.0 us)
Async XLA Ops:
  99.1 81.6 %copy-start.3 = (s32[640]{0:T(1024)S(1)}, s32[640]{0:T(1024)}, u32[]{:S(2)}) copy-start(s32[640]{0:T(1024)} %param.5) | copy-start | bytes 7684
  177.0 66.3 %all-to-all-start = ((f16[16,160,640]{2,1,0:T(8,128)(2,1)}), f16[16,160,640]{2,1,0:T(8,128)(2,1)S(1)}, u32[]{:S(2)}, u32[]{:S(2)}) async-start(f16[16,160,640]{2,1,0:T(8,128)(2,1)} %get-tuple-element.15), calls=%async_computation | async-start | bytes 6553600 | tf_op jit(solution)/shard_map/all_to_all | solution.py:50
  187.3 9.4 %copy-start.2 = (f16[16,160,640]{2,1,0:T(8,128)(2,1)S(1)}, f16[16,160,640]{2,1,0:T(8,128)(2,1)}, u32[]{:S(2)}) copy-start(f16[16,160,640]{2,1,0:T(8,128)(2,1)} %all_to_all.31) | copy-start | bytes 9830404
  243.3 1.7 copy-start.1
  245.0 77.8 %all-to-all-start.3 = ((bf16[16,160,640]{2,1,0:T(8,128)(2,1)}), bf16[16,160,640]{2,1,0:T(8,128)(2,1)S(1)}, u32[]{:S(2)}, u32[]{:S(2)}) async-start(bf16[16,160,640]{2,1,0:T(8,128)(2,1)} %bitcast.40), calls=%async_computation.3 | async-start | bytes 6553600 | tf_op jit(solution)/shard_map/all_to_all | solution.py:57
  322.8 77.7 %all-to-all-start.1 = ((bf16[16,160,640]{2,1,0:T(8,128)(2,1)}), bf16[16,160,640]{2,1,0:T(8,128)(2,1)}, u32[]{:S(2)}, u32[]{:S(2)}) async-start(bf16[16,160,640]{2,1,0:T(8,128)(2,1)} %bitcast.39), calls=%async_computation.1 | async-start | bytes 6553600 | tf_op jit(solution)/shard_map/all_to_all | solution.py:57
  400.5 77.6 %all-to-all-start.5 = ((bf16[16,160,640]{2,1,0:T(8,128)(2,1)}), bf16[16,160,640]{2,1,0:T(8,128)(2,1)}, u32[]{:S(2)}, u32[]{:S(2)}) async-start(bf16[16,160,640]{2,1,0:T(8,128)(2,1)} %bitcast.36), calls=%async_computation.5 | async-start | bytes 6553600 | tf_op jit(solution)/shard_map/all_to_all | solution.py:57
  415.1 235.9 %reduce-scatter.2.cloned.1.call-start = ((), (), s32[]{:S(2)}) async-start(), calls=%async_computation.7 | async-start | bytes 32440320 | tf_op jit(solution)/shard_map/reduce_scatter | solution.py:78
  462.5 11.4 %copy-start = (bf16[16,40,4,640]{3,2,1,0:T(4,128)(2,1)S(1)}, bf16[16,40,4,640]{3,2,1,0:T(4,128)(2,1)}, u32[]{:S(2)}) copy-start(bf16[16,40,4,640]{3,2,1,0:T(4,128)(2,1)} %reshape_transpose_reshape.10) | copy-start | bytes 9830404
Sparse Core Ops, SparseCore 0:
  610.7 40.3 reduce-scatter.1
